TPU v7x, 32 devices: a whole 2x2x4 slice. The times are simulated.
32 devices in a mesh: tracer: 2 (over core), dev: 16 (over z, y, x).
Axes of the slice: x: 2, y: 2, z: 4, core: 2. Of those that a mesh axis runs over, the one named last changes fastest.
Arguments:
- coeffs: bfloat16 [2, 256, 32, 2047], P('tracer', 'dev'), may hold values from -6 to 6
- bessel: bfloat16 [2, 1536, 512, 256], P('tracer', 'dev'), may hold values from -0.375 to 0.375
- azimuthal_order_slots: int32 [16], replicated, may hold values from 0 to 1440, as said below
Outputs:
- cross: float32 [2, 768, 512, 512], P('tracer', 'dev')
Inputs may be any that keep to these rules, and one draw needn't show every extreme that they name: `azimuthal_order_slots`: the 16 values are exactly the multiples k * (96) for k = 0 .. 15, each once, in an order drawn from the seed.
All inputs are finite; a program needn't handle non-finite values.
Results may differ from a plain program's by a relative error of at most 0.008.
Values may be sent and summed in bfloat16 or wider, within the bound.
A program may use at most 128 MiB of HBM per device.

v0:
```python
import jax
import jax.numpy as jnp
from jax import lax
from jax.sharding import PartitionSpec as P

NSIDE = 512
CYCLES = 2047
LMAX = 1536
SHELLS = 256
M_DEV = 1
LB = 128


rescale_limit = 10000000000.0


def swapped(value, axis, apart):
    mask = 2**apart
    pairs = [(source, source ^ mask) for source in range(lax.axis_size(axis))]
    return lax.ppermute(value, axis, pairs)


def cycle_geometry():
    cycle_number = jnp.arange(1, CYCLES + 1, dtype=jnp.float32)
    nside_float = jnp.float32(NSIDE)
    folded = jnp.minimum(cycle_number, 4.0 * nside_float - cycle_number)
    polar_cycle = folded < nside_float
    polar_gap = folded * folded / (3.0 * nside_float * nside_float)
    equator_height = 4.0 / 3.0 - 2.0 * folded / (3.0 * nside_float)
    cycle_height = jnp.where(polar_cycle, 1.0 - polar_gap, equator_height)
    height_gap = jnp.where(polar_cycle, polar_gap, 1.0 - equator_height)
    sine_cycle = jnp.sqrt(height_gap * (1.0 + cycle_height))
    cosine_latitude = jnp.where(cycle_number <= 2.0 * nside_float, cycle_height, -cycle_height)
    pixels = jnp.where(polar_cycle, 4.0 * folded, 4.0 * nside_float)
    weight = jnp.sqrt(jnp.pi * pixels / (3.0 * nside_float * nside_float))
    return (cosine_latitude, sine_cycle, weight)


def legendre_seed(orders, sine_cycle):
    counter = jnp.arange(1, LMAX + 1, dtype=jnp.float32)
    log_terms = jnp.log1p(-0.5 / counter)
    partial_sum = jnp.sum(
        jnp.where(counter[None, :] <= orders[:, None], log_terms[None, :], 0.0), axis=1
    )
    head = 0.5 * jnp.log((2.0 * orders + 1.0) / (4.0 * jnp.pi)) + 0.5 * partial_sum
    return head[:, None] + orders[:, None] * jnp.log(sine_cycle)[None, :]


def recurrence_step(carried, degree, orders, cosine_latitude, seed_log):
    previous, current, log_scale = carried
    order_col = orders[:, None]
    alpha_coef = jnp.sqrt(
        jnp.maximum(4.0 * degree * degree - 1.0, 1.0)
        / jnp.maximum(degree * degree - order_col * order_col, 1.0)
    )
    degree_below = degree - 1.0
    beta_coef = jnp.sqrt(
        jnp.maximum(degree_below * degree_below - order_col * order_col, 0.0)
        / jnp.maximum(4.0 * degree_below * degree_below - 1.0, 1.0)
    )
    starting_degree = degree == order_col
    updated = jnp.where(
        starting_degree,
        1.0,
        alpha_coef * (cosine_latitude[None, :] * current - beta_coef * previous),
    )
    previous = jnp.where(starting_degree, 0.0, current)
    log_scale = jnp.where(starting_degree, seed_log, log_scale)
    table_value = jnp.where(degree >= order_col, updated * jnp.exp(log_scale), 0.0)
    largest = jnp.maximum(jnp.abs(updated), jnp.abs(previous))
    oversized = largest > rescale_limit
    factor = jnp.where(oversized, 1.0 / jnp.maximum(largest, 1.0), 1.0)
    log_scale = log_scale + jnp.where(oversized, jnp.log(jnp.maximum(largest, 1.0)), 0.0)
    return ((previous * factor, updated * factor, log_scale), table_value)


def legendre_block(carried, first_degree, orders, cosine_latitude, seed_log, weight):

    def advance(inner_state, offset):
        degree = (first_degree + offset).astype(jnp.float32)
        return recurrence_step(inner_state, degree, orders, cosine_latitude, seed_log)

    carried, values = lax.scan(advance, carried, jnp.arange(LB, dtype=jnp.int32), unroll=8)
    return (carried, (values * weight[None, None, :]).astype(jnp.bfloat16))


def per_device(coeffs, bessel, azimuthal_order_slots):
    cosine_latitude, sine_cycle, weight = cycle_geometry()
    device = lax.axis_index("dev")
    local_orders = lax.dynamic_slice_in_dim(azimuthal_order_slots, device * M_DEV, M_DEV)
    orders = local_orders.astype(jnp.float32)
    seed_log = legendre_seed(orders, sine_cycle)
    regrouped = lax.all_to_all(coeffs[0], "dev", split_axis=1, concat_axis=0, tiled=True)
    grouped_coefficients = regrouped.reshape(SHELLS, M_DEV, 2, CYCLES)
    zero_rows = jnp.zeros((M_DEV, CYCLES), jnp.float32)
    harmonic = jnp.zeros((M_DEV, 2, LMAX, SHELLS), jnp.bfloat16)

    def fill_block(block_index, packed):
        carried, harmonic_now = packed
        carried, weighted_harmonics = legendre_block(
            carried, block_index * LB, orders, cosine_latitude, seed_log, weight
        )
        block_terms = jnp.einsum(
            "jhq,vhyq->hyjv",
            weighted_harmonics,
            grouped_coefficients,
            preferred_element_type=jnp.float32,
        ).astype(jnp.bfloat16)
        harmonic_now = lax.dynamic_update_slice_in_dim(
            harmonic_now, block_terms, block_index * LB, 2
        )
        return (carried, harmonic_now)

    first_block = 0
    final_state, harmonic = lax.fori_loop(
        first_block, LMAX // LB, fill_block, ((zero_rows, zero_rows, zero_rows), harmonic)
    )
    by_degree = lax.all_to_all(
        harmonic.reshape(2 * M_DEV, LMAX, SHELLS), "dev", split_axis=1, concat_axis=0, tiled=True
    )
    radial = jnp.einsum(
        "cls,lks->lck", by_degree, bessel[0], preferred_element_type=jnp.float32
    ).astype(jnp.bfloat16)
    degrees_here = by_degree.shape[1]
    half_depth = degrees_here // 2
    tracer_id = lax.axis_index("tracer")
    own_half = lax.dynamic_slice_in_dim(radial, tracer_id * half_depth, half_depth, 0)
    outgoing = lax.dynamic_slice_in_dim(radial, (1 - tracer_id) * half_depth, half_depth, 0)
    other_half = swapped(outgoing, "tracer", 0)
    leading = jnp.where(tracer_id == 0, own_half, other_half)
    trailing = jnp.where(tracer_id == 0, other_half, own_half)
    degree_values = (
        device * degrees_here + tracer_id * half_depth + jnp.arange(half_depth, dtype=jnp.int32)
    )
    mode_tallies = jnp.sum(
        (azimuthal_order_slots[None, :] <= degree_values[:, None]).astype(jnp.int32), axis=1
    )
    factor = 1.0 / jnp.sqrt(2.0 * mode_tallies.astype(jnp.float32))
    cross_power_spectrum = (
        jnp.einsum("lck,lcj->lkj", leading, trailing, preferred_element_type=jnp.float32)
        * factor[:, None, None]
    )
    return cross_power_spectrum[None]


def solution(mesh):
    placed = (P("tracer", "dev", None, None), P("tracer", "dev", None, None), P())
    return jax.shard_map(
        per_device,
        mesh=mesh,
        in_specs=placed,
        out_specs=P("tracer", "dev", None, None),
        check_vma=False,
    )
```

profile of v0, /device:TPU:0, one launch (start us, length us, event | category | flops | bytes accessed | tf_op | source)
XLA Modules:
  0.0 1689.4 jit_solution(16361210930652989071)
XLA Ops:
  0.0 4.1 copy.27
  4.1 8.4 all-to-all-start
  12.5 0.6 dynamic_slice.16
  15.0 40.6 %all-to-all-done = bf16[16,32,2047]{2,0,1:T(8,128)(2,1)S(1)} async-done(((bf16[16,32,2047]{2,0,1:T(8,128)(2,1)}), bf16[16,32,2047]{2,0,1:T(8,128)(2,1)S(1)}, u32[]{:S(2)}, u32[]{:S(2)}) %all-to-all-start) | async-done | bytes 2096160 | tf_op jit(solution)/shard_map/all_to_all | solution.py:93
  55.6 1.3 copy-done
  56.9 1.8 copy.16
  58.8 2.1 broadcast_in_dim.399.clone
  60.9 1544.0 %while.76 = (s32[]{:T(128)}, f32[1,2047]{1,0:T(1,128)S(1)}, f32[1,2047]{1,0:T(1,128)S(1)}, f32[1,2047]{1,0:T(1,128)S(1)}, bf16[1,2,1536,256]{3,1,2,0:T(2,128)(2,...) while((s32[]{:T(128)}, f32[1,2047]{1,0:T(1,128)S(1)}, ...), condition=%wide.region_4.5_spmd.clone.clone, body=%wide.region_1.4_spmd.clone.clone.sunk | while | flops 269375424 | bytes 4482748 | solution.py:115
  61.0 126.9 %while.77 = (s32[]{:T(128)}, f32[1,2047]{1,0:T(1,128)S(1)}, f32[1,2047]{1,0:T(1,128)S(1)}, f32[1,2047]{1,0:T(1,128)S(1)}, f32[16,8,1,2047]{3,1,0,2:T(8,128)S(1)}...) while((s32[]{:T(128)}, f32[1,2047]{1,0:T(1,128)S(1)}, ...), condition=%wide.region_3.3_spmd.clone, body=%wide.region_2.2_spmd.clone.sunk | while | flops 407522 | bytes 911693 | solution.py:83
  69.1 0.6 fusion.62
  100.8 0.6 fusion.62
  124.6 0.6 fusion.62
  132.5 0.6 fusion.62
  156.3 0.6 fusion.62
  164.2 0.6 fusion.62
  188.0 0.8 fusion.61
  188.8 0.8 copy_dynamic-update-slice_fusion.4
  189.7 126.9 %while.77 = (s32[]{:T(128)}, f32[1,2047]{1,0:T(1,128)S(1)}, f32[1,2047]{1,0:T(1,128)S(1)}, f32[1,2047]{1,0:T(1,128)S(1)}, f32[16,8,1,2047]{3,1,0,2:T(8,128)S(1)}...) while((s32[]{:T(128)}, f32[1,2047]{1,0:T(1,128)S(1)}, ...), condition=%wide.region_3.3_spmd.clone, body=%wide.region_2.2_spmd.clone.sunk | while | flops 407522 | bytes 911693 | solution.py:83
  197.7 0.6 fusion.62
  205.7 0.6 fusion.62
  229.4 0.6 fusion.62
  237.4 0.6 fusion.62
  261.2 0.6 fusion.62
  269.1 0.6 fusion.62
  316.6 0.8 fusion.61
  317.4 0.8 copy_dynamic-update-slice_fusion.4
  318.4 126.9 %while.77 = (s32[]{:T(128)}, f32[1,2047]{1,0:T(1,128)S(1)}, f32[1,2047]{1,0:T(1,128)S(1)}, f32[1,2047]{1,0:T(1,128)S(1)}, f32[16,8,1,2047]{3,1,0,2:T(8,128)S(1)}...) while((s32[]{:T(128)}, f32[1,2047]{1,0:T(1,128)S(1)}, ...), condition=%wide.region_3.3_spmd.clone, body=%wide.region_2.2_spmd.clone.sunk | while | flops 407522 | bytes 911693 | solution.py:83
  445.3 0.8 fusion.61
  446.1 0.8 copy_dynamic-update-slice_fusion.4
  447.0 126.9 %while.77 = (s32[]{:T(128)}, f32[1,2047]{1,0:T(1,128)S(1)}, f32[1,2047]{1,0:T(1,128)S(1)}, f32[1,2047]{1,0:T(1,128)S(1)}, f32[16,8,1,2047]{3,1,0,2:T(8,128)S(1)}...) while((s32[]{:T(128)}, f32[1,2047]{1,0:T(1,128)S(1)}, ...), condition=%wide.region_3.3_spmd.clone, body=%wide.region_2.2_spmd.clone.sunk | while | flops 407522 | bytes 911693 | solution.py:83
  574.0 0.8 fusion.61
  574.8 0.8 copy_dynamic-update-slice_fusion.4
  575.7 126.9 %while.77 = (s32[]{:T(128)}, f32[1,2047]{1,0:T(1,128)S(1)}, f32[1,2047]{1,0:T(1,128)S(1)}, f32[1,2047]{1,0:T(1,128)S(1)}, f32[16,8,1,2047]{3,1,0,2:T(8,128)S(1)}...) while((s32[]{:T(128)}, f32[1,2047]{1,0:T(1,128)S(1)}, ...), condition=%wide.region_3.3_spmd.clone, body=%wide.region_2.2_spmd.clone.sunk | while | flops 407522 | bytes 911693 | solution.py:83
  702.6 0.8 fusion.61
  703.4 0.8 copy_dynamic-update-slice_fusion.4
  704.4 126.9 %while.77 = (s32[]{:T(128)}, f32[1,2047]{1,0:T(1,128)S(1)}, f32[1,2047]{1,0:T(1,128)S(1)}, f32[1,2047]{1,0:T(1,128)S(1)}, f32[16,8,1,2047]{3,1,0,2:T(8,128)S(1)}...) while((s32[]{:T(128)}, f32[1,2047]{1,0:T(1,128)S(1)}, ...), condition=%wide.region_3.3_spmd.clone, body=%wide.region_2.2_spmd.clone.sunk | while | flops 407522 | bytes 911693 | solution.py:83
  831.3 0.8 fusion.61
  832.1 0.8 copy_dynamic-update-slice_fusion.4
  833.0 126.9 %while.77 = (s32[]{:T(128)}, f32[1,2047]{1,0:T(1,128)S(1)}, f32[1,2047]{1,0:T(1,128)S(1)}, f32[1,2047]{1,0:T(1,128)S(1)}, f32[16,8,1,2047]{3,1,0,2:T(8,128)S(1)}...) while((s32[]{:T(128)}, f32[1,2047]{1,0:T(1,128)S(1)}, ...), condition=%wide.region_3.3_spmd.clone, body=%wide.region_2.2_spmd.clone.sunk | while | flops 407522 | bytes 911693 | solution.py:83
  959.9 0.8 fusion.61
  960.8 0.8 copy_dynamic-update-slice_fusion.4
  961.7 126.9 %while.77 = (s32[]{:T(128)}, f32[1,2047]{1,0:T(1,128)S(1)}, f32[1,2047]{1,0:T(1,128)S(1)}, f32[1,2047]{1,0:T(1,128)S(1)}, f32[16,8,1,2047]{3,1,0,2:T(8,128)S(1)}...) while((s32[]{:T(128)}, f32[1,2047]{1,0:T(1,128)S(1)}, ...), condition=%wide.region_3.3_spmd.clone, body=%wide.region_2.2_spmd.clone.sunk | while | flops 407522 | bytes 911693 | solution.py:83
  1088.6 0.8 fusion.61
  1089.4 0.8 copy_dynamic-update-slice_fusion.4
  1090.4 126.9 %while.77 = (s32[]{:T(128)}, f32[1,2047]{1,0:T(1,128)S(1)}, f32[1,2047]{1,0:T(1,128)S(1)}, f32[1,2047]{1,0:T(1,128)S(1)}, f32[16,8,1,2047]{3,1,0,2:T(8,128)S(1)}...) while((s32[]{:T(128)}, f32[1,2047]{1,0:T(1,128)S(1)}, ...), condition=%wide.region_3.3_spmd.clone, body=%wide.region_2.2_spmd.clone.sunk | while | flops 407522 | bytes 911693 | solution.py:83
  1217.3 0.8 fusion.61
  1218.1 0.8 copy_dynamic-update-slice_fusion.4
  1219.0 126.9 %while.77 = (s32[]{:T(128)}, f32[1,2047]{1,0:T(1,128)S(1)}, f32[1,2047]{1,0:T(1,128)S(1)}, f32[1,2047]{1,0:T(1,128)S(1)}, f32[16,8,1,2047]{3,1,0,2:T(8,128)S(1)}...) while((s32[]{:T(128)}, f32[1,2047]{1,0:T(1,128)S(1)}, ...), condition=%wide.region_3.3_spmd.clone, body=%wide.region_2.2_spmd.clone.sunk | while | flops 407522 | bytes 911693 | solution.py:83
  1345.9 0.8 fusion.61
  1346.8 0.8 copy_dynamic-update-slice_fusion.4
  1347.7 126.9 %while.77 = (s32[]{:T(128)}, f32[1,2047]{1,0:T(1,128)S(1)}, f32[1,2047]{1,0:T(1,128)S(1)}, f32[1,2047]{1,0:T(1,128)S(1)}, f32[16,8,1,2047]{3,1,0,2:T(8,128)S(1)}...) while((s32[]{:T(128)}, f32[1,2047]{1,0:T(1,128)S(1)}, ...), condition=%wide.region_3.3_spmd.clone, body=%wide.region_2.2_spmd.clone.sunk | while | flops 407522 | bytes 911693 | solution.py:83
  1474.6 0.8 fusion.61
  1475.4 0.8 copy_dynamic-update-slice_fusion.4
  1476.4 126.9 %while.77 = (s32[]{:T(128)}, f32[1,2047]{1,0:T(1,128)S(1)}, f32[1,2047]{1,0:T(1,128)S(1)}, f32[1,2047]{1,0:T(1,128)S(1)}, f32[16,8,1,2047]{3,1,0,2:T(8,128)S(1)}...) while((s32[]{:T(128)}, f32[1,2047]{1,0:T(1,128)S(1)}, ...), condition=%wide.region_3.3_spmd.clone, body=%wide.region_2.2_spmd.clone.sunk | while | flops 407522 | bytes 911693 | solution.py:83
  1603.3 0.8 fusion.61
  1604.1 0.8 copy_dynamic-update-slice_fusion.4
  1604.9 10.0 all-to-all-start.1
  1614.9 33.5 %all-to-all-done.1 = bf16[2,1536,256]{2,0,1:T(2,128)(2,1)S(1)} async-done(((bf16[2,1536,256]{2,0,1:T(2,128)(2,1)}), bf16[2,1536,256]{2,0,1:T(2,128)(2,1)S(1)}, u32[]{:S(2)}, u32[]{:S(2)}) %all-to-all-start.1) | async-done | bytes 1572896 | tf_op jit(solution)/shard_map/all_to_all | solution.py:118
  1648.4 1.7 copy.28
  1650.2 0.6 all_to_all.30
  1650.8 13.2 fusion.40
  1664.1 1.6 constant_dynamic-slice_fusion.1
  1665.9 3.3 collective-permute-done
  1669.1 20.3 %multiply_bitcast_fusion = f32[1,48,512,512]{3,2,1,0:T(8,128)} fusion(f32[48]{0:T(128)S(1)} %multiply_rsqrt_fusion, bf16[48,32,512]{2,1,0:T(8,128)(2,1)S(1)} %collective-permute-done, bf16[96,32,512]{2,1,0:T(8,128)(2,1)} %fusion.40, s32[]{:T(128)S(6)} %select_n.398, pred[]{:T(512)S(6)} %eq.100), kind=kOutput, calls=%fused_computation.107 | convolution fusion | flops 819462144 | bytes 56625664 | tf_op jit(solution)/shard_map/lck,lcj->lkj/dot_general | solution.py:140
  (2747 shorter events, 272.8 us)
Async XLA Ops:
  4.1 8.5 copy-start.1
  4.1 51.5 %all-to-all-start = ((bf16[16,32,2047]{2,0,1:T(8,128)(2,1)}), bf16[16,32,2047]{2,0,1:T(8,128)(2,1)S(1)}, u32[]{:S(2)}, u32[]{:S(2)}) async-start(bf16[16,32,2047]{2,0,1:T(8,128)(2,1)} %bitcast.358), calls=%async_computation | async-start | bytes 4194304 | tf_op jit(solution)/shard_map/all_to_all | solution.py:93
  55.6 1.3 copy-start
  1604.9 43.5 %all-to-all-start.1 = ((bf16[2,1536,256]{2,0,1:T(2,128)(2,1)}), bf16[2,1536,256]{2,0,1:T(2,128)(2,1)S(1)}, u32[]{:S(2)}, u32[]{:S(2)}) async-start(bf16[2,1536,256]{2,0,1:T(2,128)(2,1)} %bitcast.360), calls=%async_computation.1 | async-start | bytes 3145728 | tf_op jit(solution)/shard_map/all_to_all | solution.py:118
  1665.7 3.5 collective-permute-start
where the time goes:
time: 1710 us; the launch traced here: 1690 us
  loops' own time  1250 us (73%)
  local copies, waits for them, and re-layouts  157 us (9%)
  other arithmetic  146 us (9%)
  waiting for transfers between devices  77.4 us (5%)
  matrix products  43.3 us (3%)
  starting transfers between devices  18.5 us (1%)
    another operation x12, loops' own time, legendre_block(): lax.scan(advance, carried, jnp.arange(LB, dtype=jnp.int32), unroll=8)  1250 us
    slice x192, local copies, waits for them, and re-layouts, legendre_block(): lax.scan(advance, carried, jnp.arange(LB, dtype=jnp.int32), unroll=8)  115 us
    while x1344, other arithmetic  111 us
    all_to_all x1, waiting for transfers between devices, per_device(): lax.all_to_all(coeffs[0], 'dev', split_axis=1, concat_axis=0, tiled=True)  40.6 us
  transfers between devices with their start and end apart: 3, of which 3 were waited for; matrix products, arithmetic and copies ran while one was open for 0% of the time, Pallas kernels for 0%

commit v1 on v0

v1 whole, which is shorter than its diff:
```python
import functools

import jax
import jax.numpy as jnp
from jax import lax
from jax.experimental import pallas as pl
from jax.experimental.pallas import tpu as pltpu
from jax.sharding import PartitionSpec as P

RESCALE_LIMIT = 1e10
LANES = 128
GROUP = 2


def north_geometry(nside):
    folded = jnp.arange(1, 2 * nside + 1, dtype=jnp.float32)
    nside_float = jnp.float32(nside)
    polar_cycle = folded < nside_float
    polar_gap = folded * folded / (3.0 * nside_float * nside_float)
    equator_height = 4.0 / 3.0 - 2.0 * folded / (3.0 * nside_float)
    cosine = jnp.where(polar_cycle, 1.0 - polar_gap, equator_height)
    height_gap = jnp.where(polar_cycle, polar_gap, 1.0 - equator_height)
    sine = jnp.sqrt(height_gap * (1.0 + cosine))
    pixels = jnp.where(polar_cycle, 4.0 * folded, 4.0 * nside_float)
    weight = jnp.sqrt(jnp.pi * pixels / (3.0 * nside_float * nside_float))
    return cosine, sine, weight


def legendre_seed(orders, sine, lmax):
    counter = jnp.arange(1, lmax + 1, dtype=jnp.float32)
    log_terms = jnp.log1p(-0.5 / counter)
    partial_sum = jnp.sum(
        jnp.where(counter[None, :] <= orders[:, None], log_terms[None, :], 0.0), axis=1
    )
    head = 0.5 * jnp.log((2.0 * orders + 1.0) / (4.0 * jnp.pi)) + 0.5 * partial_sum
    return head[:, None] + orders[:, None] * jnp.log(sine)[None, :]


def recurrence_coefficients(orders, lmax):
    degree = jnp.arange(lmax, dtype=jnp.float32)[None, :]
    order_col = orders[:, None]
    alpha = jnp.sqrt(
        jnp.maximum(4.0 * degree * degree - 1.0, 1.0)
        / jnp.maximum(degree * degree - order_col * order_col, 1.0)
    )
    below = degree - 1.0
    beta = jnp.sqrt(
        jnp.maximum(below * below - order_col * order_col, 0.0)
        / jnp.maximum(4.0 * below * below - 1.0, 1.0)
    )
    starting = degree == order_col
    return jnp.where(starting, 1.0, alpha), jnp.where(starting, 1.0, beta)


def harmonic_kernel(lines, slots, lb, unroll, alpha_ref, beta_ref, cosine_ref, weight_ref,
                    seed_ref, coef_ref, out_ref, prev_ref, cur_ref, log_ref, scale_ref, table):
    block = pl.program_id(0)
    half = lax.axis_index("tracer")
    rows = cosine_ref.shape[0]
    part = coef_ref.shape[1] // 2

    @pl.when(block == 0)
    def _():
        for ref in (prev_ref, cur_ref, log_ref, scale_ref):
            ref[...] = jnp.zeros_like(ref)

    out_ref[...] = jnp.zeros_like(out_ref)
    cosine = cosine_ref[...]
    weight = weight_ref[...]
    active = (block - half + lines) // lines

    def group(g, carry):
        picks = [g * GROUP + i for i in range(GROUP)]
        state = []
        for p in picks:
            starting = p * lines + half == block
            log_scale = jnp.where(starting, seed_ref[p], log_ref[p])
            scale = jnp.where(starting, jnp.exp(log_scale) * weight, scale_ref[p])
            state.append((jnp.where(starting, -1.0, prev_ref[p]), cur_ref[p], log_scale, scale))

        def chunk(c, state):
            state = list(state)
            for u in range(unroll):
                offset = c * unroll + u
                for i, p in enumerate(picks):
                    prev, cur, log_scale, scale = state[i]
                    a = alpha_ref[0, 0, p * lb + offset]
                    b = beta_ref[0, 0, p * lb + offset]
                    new = a * (cosine * cur - b * prev)
                    table[i, pl.ds(pl.multiple_of(offset * rows, rows), rows), :] = new * scale
                    state[i] = (cur, new, log_scale, scale)
            for i in range(GROUP):
                prev, cur, log_scale, scale = state[i]
                largest = jnp.maximum(jnp.abs(prev), jnp.abs(cur))
                oversized = largest > RESCALE_LIMIT
                safe = jnp.maximum(largest, 1.0)
                factor = jnp.where(oversized, 1.0 / safe, 1.0)
                log_scale = log_scale + jnp.where(oversized, jnp.log(safe), 0.0)
                state[i] = (prev * factor, cur * factor, log_scale, jnp.exp(log_scale) * weight)
            return tuple(state)

        state = lax.fori_loop(0, lb // unroll, chunk, tuple(state))
        for i, p in enumerate(picks):
            prev_ref[p], cur_ref[p], log_ref[p], scale_ref[p] = state[i]
            values = jnp.concatenate(
                [table[i, pl.ds(s, lb, stride=rows), :].astype(jnp.bfloat16) for s in range(rows)],
                axis=1,
            )
            both = lax.dot_general(
                coef_ref[p], values, (((1,), (1,)), ((), ())), preferred_element_type=jnp.float32
            )
            offset = lax.broadcasted_iota(jnp.int32, (part, lb), 1)
            odd = (offset + (block + p * lines + half) * lb) % 2 == 1
            chosen = jnp.where(odd, both[part:], both[:part]).astype(jnp.bfloat16)
            each = part // lines
            for t in range(lines):
                out_ref[t, 0, p] = chosen[t * each:(t + 1) * each]
        return carry

    lax.fori_loop(0, (active + GROUP - 1) // GROUP, group, 0)


def harmonic_blocks(alpha, beta, cosine, weight, seed, coefficients, lines):
    blocks, slots, lb = alpha.shape[0], seed.shape[0], alpha.shape[2] // seed.shape[0]
    north = seed.shape[1] * LANES
    each = coefficients.shape[1] // (2 * lines)
    unroll = max(u for u in range(1, 9) if lb % u == 0)
    rows = north // LANES
    whole = lambda x: pl.BlockSpec(x.shape, lambda b: (0,) * x.ndim)
    scalar = pl.BlockSpec((1, 1, slots * lb), lambda b: (b, 0, 0), memory_space=pltpu.SMEM)
    return pl.pallas_call(
        functools.partial(harmonic_kernel, lines, slots, lb, unroll),
        grid=(blocks,),
        out_shape=jax.ShapeDtypeStruct((lines, blocks, slots, each, lb), jnp.bfloat16),
        in_specs=[scalar, scalar, whole(cosine), whole(weight), whole(seed), whole(coefficients)],
        out_specs=pl.BlockSpec((lines, 1, slots, each, lb), lambda b: (0, b, 0, 0, 0)),
        scratch_shapes=[pltpu.VMEM((slots, rows, LANES), jnp.float32)] * 4
        + [pltpu.VMEM((GROUP, lb * rows, LANES), jnp.float32)],
        compiler_params=pltpu.CompilerParams(vmem_limit_bytes=40 * 2**20),
    )(alpha, beta, cosine, weight, seed, coefficients)


def per_device(coeffs, bessel, azimuthal_order_slots):
    lines, devices = lax.axis_size("tracer"), lax.axis_size("dev")
    tracer_id, device = lax.axis_index("tracer"), lax.axis_index("dev")
    _, shells, _, cycles = coeffs.shape
    window = azimuthal_order_slots.shape[0]
    degrees_here = bessel.shape[1]
    lmax = degrees_here * devices
    stride = lmax // window
    nside = (cycles + 1) // 4
    north = 2 * nside
    slots = window // lines

    ranks = jnp.arange(window, dtype=jnp.int32)
    placed = azimuthal_order_slots[None, :] == ranks[:, None] * stride
    placed = jnp.kron(placed.astype(jnp.bfloat16), jnp.eye(2, dtype=jnp.bfloat16))
    rows = jnp.einsum("ij,sjr->isr", placed, coeffs[0], preferred_element_type=jnp.bfloat16)
    rows = rows.reshape(slots, lines, 2 * shells, cycles)
    rows = lax.all_to_all(rows, "tracer", split_axis=1, concat_axis=1, tiled=True)
    rows = rows.reshape(slots, lines * 2 * shells, cycles)
    near = rows[..., :north].astype(jnp.float32)
    far = jnp.pad(rows[..., north:], ((0, 0), (0, 0), (0, 2 * north - cycles)))
    index = jnp.arange(north, dtype=jnp.int32)
    mirror = (index[:, None] + index[None, :] == north - 2).astype(jnp.bfloat16)
    far = jnp.einsum("pnu,uv->pnv", far, mirror, preferred_element_type=jnp.float32)
    coefficients = jnp.concatenate([near + far, near - far], axis=1).astype(jnp.bfloat16)

    cosine, sine, weight = north_geometry(nside)
    orders = ((jnp.arange(slots, dtype=jnp.int32) * lines + tracer_id) * stride).astype(jnp.float32)
    seed = legendre_seed(orders, sine, lmax).reshape(slots, -1, LANES)
    alpha, beta = recurrence_coefficients(orders, lmax)
    by_block = lambda x: x.reshape(slots, window, stride).transpose(1, 0, 2).reshape(window, 1, -1)
    harmonic = harmonic_blocks(
        by_block(alpha), by_block(beta), cosine.reshape(-1, LANES), weight.reshape(-1, LANES),
        seed, coefficients, lines,
    )
    harmonic = harmonic.reshape(lines * devices, slots, 2, shells, stride)
    received = lax.all_to_all(
        harmonic, ("tracer", "dev"), split_axis=0, concat_axis=0, tiled=True
    ).reshape(lines, devices, slots, 2, shells, stride)
    by_degree = received.transpose(5, 0, 2, 3, 1, 4).reshape(stride, 2 * window, devices * shells)

    radial = jnp.einsum(
        "lcs,lks->lck", by_degree, bessel[0], preferred_element_type=jnp.float32
    ).astype(jnp.bfloat16)
    half_depth = degrees_here // 2
    own_half = lax.dynamic_slice_in_dim(radial, tracer_id * half_depth, half_depth, 0)
    outgoing = lax.dynamic_slice_in_dim(radial, (1 - tracer_id) * half_depth, half_depth, 0)
    other_half = lax.ppermute(outgoing, "tracer", [(0, 1), (1, 0)])
    leading = jnp.where(tracer_id == 0, own_half, other_half)
    trailing = jnp.where(tracer_id == 0, other_half, own_half)
    degree_values = (
        device * degrees_here + tracer_id * half_depth + jnp.arange(half_depth, dtype=jnp.int32)
    )
    mode_tallies = jnp.sum(
        (azimuthal_order_slots[None, :] <= degree_values[:, None]).astype(jnp.int32), axis=1
    )
    factor = 1.0 / jnp.sqrt(2.0 * mode_tallies.astype(jnp.float32))
    cross_power_spectrum = (
        jnp.einsum("lck,lcj->lkj", leading, trailing, preferred_element_type=jnp.float32)
        * factor[:, None, None]
    )
    return cross_power_spectrum[None]


def solution(mesh):
    placed = (P("tracer", "dev", None, None), P("tracer", "dev", None, None), P())
    return jax.shard_map(
        per_device,
        mesh=mesh,
        in_specs=placed,
        out_specs=P("tracer", "dev", None, None),
        check_vma=False,
    )
```

time: 1710 us -> 159 us (0.09); the launches traced: 1690 us -> 158 us
  loops' own time: 1250 us -> 0 us
  local copies, waits for them, and re-layouts: 157 us -> 12.8 us
  other arithmetic: 146 us -> 2.04 us
  Pallas kernels: 0 us -> 39.4 us
  waiting for transfers between devices: 77.4 us -> 55.6 us
    another operation x13 -> x0, loops' own time: 1250 us -> none  [the longest x12 1250 us: legendre_block(): lax.scan(advance, carried, jnp.arange(LB, dtype=jnp.int32), unroll=8)]
    slice x192 -> x1, local copies, waits for them, and re-layouts: 115 us -> 0.09 us  [per_device(): far = jnp.pad(rows[..., north:], ((0, 0), (0, 0), (0, 2 * north - cycles)))]
    while x1344 -> x0, other arithmetic: 111 us -> none
    pallas_call x0 -> x1, Pallas kernels: none -> 39.4 us  [harmonic_blocks(): pl.pallas_call(functools.partial(harmonic_kernel, lines, slots, lb, unrol...]
    all_to_all x2, waiting for transfers between devices: 74.1 us -> 52.2 us  [the longest x1 50.6 us: per_device(): lax.all_to_all(harmonic, ('tracer', 'dev'), split_axis=0, concat_axis=0,...]
    concatenate x192 -> x1, other arithmetic: 18 us -> 0.2 us  [per_device(): jnp.concatenate([near + far, near - far], axis=1).astype(jnp.bfloat16)]
  transfers between devices with their start and end apart: 3 -> 3, of which waited for: 3 -> 3; matrix products, arithmetic and copies ran while one was open for 0% -> 1% of each run, Pallas kernels for 0% -> 0%
where the time goes in v1:
time: 159 us; the launch traced here: 158 us
  waiting for transfers between devices  55.6 us (35%)
  Pallas kernels  39.4 us (25%)
  matrix products  36.1 us (23%)
  local copies, waits for them, and re-layouts  12.8 us (8%)
  starting transfers between devices  12.1 us (8%)
  other arithmetic  2.04 us (1%)
    all_to_all x1, waiting for transfers between devices, per_device(): lax.all_to_all(harmonic, ('tracer', 'dev'), split_axis=0, concat_axis=0,...  50.6 us
    pallas_call x1, Pallas kernels, harmonic_blocks(): pl.pallas_call(functools.partial(harmonic_kernel, lines, slots, lb, unrol...  39.4 us
    dot_general x1, matrix products, per_device(): jnp.einsum('lck,lcj->lkj', leading, trailing, preferred_element_type=jnp....  20.9 us
    dot_general x1, matrix products, per_device(): jnp.einsum('lcs,lks->lck', by_degree, bessel[0], preferred_element_type=j...  13.3 us
    all_to_all x1, starting transfers between devices, per_device(): lax.all_to_all(harmonic, ('tracer', 'dev'), split_axis=0, concat_axis=0,...  7.27 us
    all_to_all x1, starting transfers between devices, per_device(): lax.all_to_all(rows, 'tracer', split_axis=1, concat_axis=1, tiled=True)  4.81 us
    ppermute x1, waiting for transfers between devices, per_device(): other_half = lax.ppermute(outgoing, 'tracer', [(0, 1), (1, 0)])  3.4 us
  transfers between devices with their start and end apart: 3, of which 3 were waited for; matrix products, arithmetic and copies ran while one was open for 1% of the time, Pallas kernels for 0%

profile of v1, /device:TPU:0, one launch (start us, length us, event | category | flops | bytes accessed | tf_op | source)
XLA Modules:
  0.0 158.3 jit_solution(9372170202432931452)
XLA Ops:
  0.0 0.0 copy-start
  0.0 0.9 compare_convert_fusion
  0.9 0.1 broadcast_multiply_fusion
  1.0 0.2 reshape.363
  1.2 0.4 copy-done
  1.6 0.7 fusion.10
  2.3 1.2 copy.15
  3.5 1.6 copy.16
  5.0 4.8 %all-to-all-start = ((bf16[8,2,32,2047]{3,2,0,1:T(8,128)(2,1)}), bf16[8,2,32,2047]{3,2,0,1:T(8,128)(2,1)}, u32[]{:S(2)}, u32[]{:S(2)}) async-start(bf16[8,2,32,2047]{3,2,0,1:T(8,128)(2,1)} %copy.16), calls=%async_computation | async-start | bytes 4194304 | tf_op jit(solution)/shard_map/all_to_all | solution.py:160
  10.0 0.1 eq.95
  10.1 0.1 eq.96
  10.2 0.2 select_reduce_fusion
  10.4 0.1 sub.96
  10.5 0.1 sub.97
  10.6 0.1 div.68
  10.7 0.1 div.71
  10.8 0.1 eq.94
  11.0 0.1 sub.95
  11.1 0.1 sub.102
  11.3 1.6 all-to-all-done
  12.8 1.7 %copy.17 = bf16[8,2,32,2047]{3,2,1,0:T(8,128)(2,1)S(1)} copy(bf16[8,2,32,2047]{3,2,0,1:T(8,128)(2,1)} %all-to-all-done) | data formatting | bytes 4192256 | tf_op jit(solution)/shard_map/all_to_all | solution.py:160
  14.6 0.1 slice.9
  14.7 1.3 fusion.8
  16.0 0.1 multiply_add_fusion.seed_ref
  16.0 0.2 pad_maximum_fusion.coef_ref
  16.3 0.3 compare_select_fusion
  16.6 39.4 %shard_map.37 = bf16[2,16,8,32,96]{4,3,2,1,0:T(8,128)(2,1)} custom-call(f32[16,1,768]{2,1,0:T(1,128)S(1)} %get-tuple-element.8.alpha_ref, f32[16,1,768]{2,1,0:T(1,128)S(1)} %get-tuple-element.7.beta_ref, f32[8,128]{1,0:T(8,128)S(1)} %get-tuple-element.12.cosine_ref, f32[8,128]{1,0:T(8,128)S(1)} %get-tuple-element.11.weight_ref, ...), custom_call_target="tpu_custom_call" | custom-call | tf_op jit(solution)/shard_map/pallas_call | solution.py:131
  56.0 7.3 %all-to-all-start.1 = ((bf16[32,8,2,16,96]{4,3,2,1,0:T(8,128)(2,1)}), bf16[32,8,2,16,96]{4,3,2,1,0:T(8,128)(2,1)S(1)}, u32[]{:S(2)}, u32[]{:S(2)}) async-start(bf16[32,8,2,16,96]{4,3,2,1,0:T(8,128)(2,1)} %bitcast.4), calls=%async_computation.1 | async-start | bytes 4194304 | tf_op jit(solution)/shard_map/all_to_all | solution.py:179
  63.2 50.6 %all-to-all-done.1 = bf16[32,8,2,16,96]{4,3,2,1,0:T(8,128)(2,1)S(1)} async-done(((bf16[32,8,2,16,96]{4,3,2,1,0:T(8,128)(2,1)}), bf16[32,8,2,16,96]{4,3,2,1,0:T(8,128)(2,1)S(1)}, u32[]{:S(2)}, u32[]{:S(2)}) %all-to-all-start.1) | async-done | bytes 1572896 | tf_op jit(solution)/shard_map/all_to_all | solution.py:179
  113.9 1.9 %copy.18 = bf16[96,2,8,2,16,16]{0,5,4,3,2,1:T(8,128)(2,1)} copy(bf16[96,2,8,2,16,16]{0,5,3,2,4,1:T(8,128)(2,1)S(1)} %bitcast.27) | data formatting | bytes 3145728 | tf_op jit(solution)/shard_map/transpose | solution.py:182
  115.8 3.2 %copy.19 = bf16[96,32,256]{2,1,0:T(8,128)(2,1)S(1)} copy(bf16[96,32,256]{0,2,1:T(8,128)(2,1)} %bitcast.26) | data formatting | bytes 3145728 | tf_op jit(solution)/shard_map/reshape | solution.py:182
  118.9 13.3 %fusion.5 = bf16[96,32,512]{2,1,0:T(8,128)(2,1)} fusion(bf16[96,32,256]{2,1,0:T(8,128)(2,1)S(1)} %copy.19, bf16[1,96,512,256]{3,2,1,0:T(8,128)(2,1)} %param.4), kind=kOutput, calls=%fused_computation.8 | convolution fusion | flops 806879232 | bytes 29884416 | tf_op jit(solution)/shard_map/lcs,lks->lck/dot_general | solution.py:184
  132.2 0.0 copy-start.2
  132.2 1.6 %constant_dynamic-slice_fusion = bf16[48,32,512]{2,1,0:T(8,128)(2,1)S(1)} fusion(bf16[96,32,512]{2,1,0:T(8,128)(2,1)} %fusion.5, s32[]{:T(128)S(6)} %select_n.74), kind=kLoop, calls=%fused_computation.54 | loop fusion | bytes 3145732 | tf_op jit(solution)/shard_map/dynamic_slice | solution.py:189
  133.8 0.1 collective-permute-start
  133.9 0.0 copy-done.2
  133.9 0.1 convert_reduce_fusion
  134.0 3.4 %collective-permute-done = bf16[48,32,512]{2,1,0:T(8,128)(2,1)} collective-permute-done((bf16[48,32,512]{2,1,0:T(8,128)(2,1)S(1)}, bf16[48,32,512]{2,1,0:T(8,128)(2,1)}, u32[]{:S(2)}, u32[]{:S(2)}) %collective-permute-start) | collective-permute-done | bytes 1572896 | tf_op jit(solution)/shard_map/ppermute | solution.py:190
  137.4 0.0 copy-start.1
  137.4 20.9 %multiply_bitcast_fusion = f32[1,48,512,512]{3,2,1,0:T(8,128)} fusion(f32[48]{0:T(128)S(1)} %multiply_rsqrt_fusion, bf16[48,32,512]{2,1,0:T(8,128)(2,1)} %collective-permute-done, bf16[96,32,512]{2,1,0:T(8,128)(2,1)} %fusion.5, s32[]{:T(128)S(6)} %select_n.73, pred[]{:T(512)S(6)} %eq.89), kind=kOutput, calls=%fused_computation | convolution fusion | flops 819462144 | bytes 56625344 | tf_op jit(solution)/shard_map/lck,lcj->lkj/dot_general | solution.py:201
  158.3 0.0 copy-done.1
  (20 shorter events, 0.2 us)
Async XLA Ops:
  0.0 1.6 %copy-start = (bf16[1,16,32,2047]{3,2,1,0:T(8,128)(2,1)S(1)}, bf16[1,16,32,2047]{3,2,1,0:T(8,128)(2,1)}, u32[]{:S(2)}) copy-start(bf16[1,16,32,2047]{3,2,1,0:T(8,128)(2,1)} %param.3) | copy-start | bytes 6288388
  5.0 7.8 %all-to-all-start = ((bf16[8,2,32,2047]{3,2,0,1:T(8,128)(2,1)}), bf16[8,2,32,2047]{3,2,0,1:T(8,128)(2,1)}, u32[]{:S(2)}, u32[]{:S(2)}) async-start(bf16[8,2,32,2047]{3,2,0,1:T(8,128)(2,1)} %copy.16), calls=%async_computation | async-start | bytes 4194304 | tf_op jit(solution)/shard_map/all_to_all | solution.py:160
  56.0 57.9 %all-to-all-start.1 = ((bf16[32,8,2,16,96]{4,3,2,1,0:T(8,128)(2,1)}), bf16[32,8,2,16,96]{4,3,2,1,0:T(8,128)(2,1)S(1)}, u32[]{:S(2)}, u32[]{:S(2)}) async-start(bf16[32,8,2,16,96]{4,3,2,1,0:T(8,128)(2,1)} %bitcast.4), calls=%async_computation.1 | async-start | bytes 4194304 | tf_op jit(solution)/shard_map/all_to_all | solution.py:179
  132.2 1.7 %copy-start.2 = (s32[16]{0:T(128)S(1)}, s32[16]{0:T(128)}, u32[]{:S(2)}) copy-start(s32[16]{0:T(128)} %param.5) | copy-start | bytes 196
  133.8 3.6 %collective-permute-start = (bf16[48,32,512]{2,1,0:T(8,128)(2,1)S(1)}, bf16[48,32,512]{2,1,0:T(8,128)(2,1)}, u32[]{:S(2)}, u32[]{:S(2)}) collective-permute-start(bf16[48,32,512]{2,1,0:T(8,128)(2,1)S(1)} %constant_dynamic-slice_fusion), channel_id=1, source_target_pairs={{0,16},{16,0},{1,17},{17,1},{2,18},{18,2},{3,19},{19,3},{4,20},{20... | collective-permute-start | bytes 4718600 | tf_op jit(solution)/shard_map/ppermute | solution.py:190
  137.4 20.9 %copy-start.1 = (bf16[1,16,32,2047]{3,2,1,0:T(8,128)(2,1)S(1)}, bf16[1,16,32,2047]{3,2,1,0:T(8,128)(2,1)}, u32[]{:S(2)}) copy-start(bf16[1,16,32,2047]{3,2,1,0:T(8,128)(2,1)} %param.3) | copy-start | bytes 6288388
